TPU v7x, 32 devices: a whole 2x2x4 slice. The times are simulated.
32 devices in a mesh: groups: 2 (over y), expert: 16 (over z, x, core).
Axes of the slice: x: 2, y: 2, z: 4, core: 2. Of those that a mesh axis runs over, the one named last changes fastest.
Arguments:
- activations: bfloat16 [2, 512, 2048], P(None, ('groups', 'expert')), parts along dimension 1, may hold values from -6 to 6
- pick_weight: float32 [2, 512, 1], P(None, ('groups', 'expert')), parts along dimension 1, may hold values from 0.2 to 1
- expert_ids: int32 [2, 512, 1], P(None, ('groups', 'expert')), parts along dimension 1, may hold values from 0 to 7, as said below
- replica: int32 [2, 512, 1], P(None, ('groups', 'expert')), parts along dimension 1, may hold values from 0 to 4, as said below
- old_home: int32 [8], replicated, may hold values from 0 to 7, each once
- new_expert: int32 [32], P('groups'), parts along dimension 0, may hold values from 0 to 7, as said below
- gate_panel: bfloat16 [16, 2048, 384], P('expert'), may hold values from -0.125 to 0.125
- up_panel: bfloat16 [16, 2048, 384], P('expert'), may hold values from -0.125 to 0.125
- down_panel: bfloat16 [16, 2048, 384], P('expert'), may hold values from -0.21875 to 0.21875
Outputs:
- layer_output: bfloat16 [2, 512, 2048], P(None, ('groups', 'expert')), parts along dimension 1
- slot_load: int32 [32], P(('groups', 'expert')), parts along dimension 0
There are 2 independent parts, one for each index of `groups`. A program takes and returns all parts, laid end to end along the dimension named above; an argument that names none is the same for every part. Nothing has to cross between parts.
Inputs may be any that keep to these rules, and one draw needn't show every extreme that they name: `new_expert`: every expert is held by 1 or 5 slots. `expert_ids`: the 1 expert that a token names are different. replica[s, t, k] is below the number of slots that new_expert gives to expert_ids[s, t, k]. The picks of the 16 tokens of one device in one batch that land on one slot number at most 2, and in each batch some slot receives exactly 2 from every device.
All inputs are finite; a program needn't handle non-finite values.
Results may differ from a plain program's by a relative error of at most 0.0057.
Values may be sent and summed in bfloat16 or wider, within the bound.
A program may use at most 128 MiB of HBM per device.

v0:
```python
import jax
import jax.numpy as jnp
from jax import lax
from jax.sharding import PartitionSpec as P

CAP = 2


def slot_ranks(new_expert):
    count = new_expert.shape[0]
    positions = jnp.arange(count, dtype=jnp.int32)
    same = new_expert[:, None] == new_expert[None, :]
    earlier = positions[None, :] < positions[:, None]
    return jnp.sum((same & earlier).astype(jnp.int32), axis=1)


def expert_rows(picked, gate_full, up_full, down_full):
    gate = jnp.dot(picked, gate_full, preferred_element_type=jnp.float32)
    up_sum = jnp.dot(picked, up_full, preferred_element_type=jnp.float32)
    hidden = (jax.nn.silu(gate) * up_sum).astype(jnp.bfloat16)
    result = lax.dot_general(
        hidden, down_full, (((1,), (1,)), ((), ())), preferred_element_type=jnp.float32
    )
    return result.astype(jnp.bfloat16)


def route(tokens, ids, replica, new_expert, ranks):
    slots = new_expert.shape[0]
    per_token = ids.shape[1]
    picks = ids.shape[0] * per_token
    flat_ids = ids.reshape(picks)
    flat_rep = replica.reshape(picks)
    match = (new_expert[None, :] == flat_ids[:, None]) & (ranks[None, :] == flat_rep[:, None])
    match_int = match.astype(jnp.int32)
    slot_index = jnp.sum(match_int * jnp.arange(slots, dtype=jnp.int32)[None, :], axis=1)
    before = jnp.cumsum(match_int, axis=0) - match_int
    position = jnp.sum(before * match_int, axis=1)
    target = slot_index * CAP + position
    places = jnp.arange(slots * CAP, dtype=jnp.int32)
    chosen = (target[None, :] == places[:, None]).astype(jnp.int32)
    live = jnp.sum(chosen, axis=1)
    owner = jnp.arange(picks, dtype=jnp.int32) // per_token
    source = jnp.sum(chosen * owner[None, :], axis=1)
    sent = jnp.where(live[:, None] > 0, tokens[source], jnp.zeros((), tokens.dtype))
    return (sent.reshape(slots, CAP, tokens.shape[1]), live.reshape(slots, CAP), target)


def combine(back, target, weights):
    flat = back.reshape(-1, back.shape[-1])
    picked = flat[target].reshape(weights.shape[0], weights.shape[1], -1)
    total = jnp.sum(weights[:, :, None] * picked.astype(jnp.float32), axis=1)
    return total.astype(jnp.bfloat16)


def per_device(
    activations,
    pick_weight,
    expert_ids,
    replica,
    old_home,
    new_expert,
    gate_panel,
    up_panel,
    down_panel,
):
    slots = lax.axis_size("expert")
    width = gate_panel.shape[1]
    half = gate_panel.shape[2]
    block = width // slots
    ranks = slot_ranks(new_expert)
    batches = activations.shape[0]
    routed = [
        route(activations[batch], expert_ids[batch], replica[batch], new_expert, ranks)
        for batch in range(batches)
    ]
    sent_all = jnp.concatenate([item[0] for item in routed], axis=1)
    live_all = jnp.concatenate([item[1] for item in routed], axis=1)
    early_cells, early_marks = (
        lax.all_to_all(sent_all, "expert", split_axis=0, concat_axis=0, tiled=True),
        lax.all_to_all(live_all, "expert", split_axis=0, concat_axis=0, tiled=True),
    )
    gate_rows, up_rows, down_rows = (
        lax.all_to_all(
            gate_panel.reshape(slots, block, half),
            "expert",
            split_axis=0,
            concat_axis=0,
            tiled=True,
        ),
        lax.all_to_all(
            up_panel.reshape(slots, block, half), "expert", split_axis=0, concat_axis=0, tiled=True
        ),
        lax.all_to_all(
            down_panel.reshape(slots, block, half),
            "expert",
            split_axis=0,
            concat_axis=0,
            tiled=True,
        ),
    )
    labels = jnp.arange(old_home.shape[0], dtype=jnp.int32)
    home = jnp.sum(
        (new_expert[:, None] == labels[None, :]).astype(jnp.int32) * old_home[None, :], axis=1
    )
    first = 2 * home
    second = first + 1

    def deliver(pieces):
        return jnp.stack(
            (jnp.take(pieces, first, axis=0), jnp.take(pieces, second, axis=0)), axis=2
        )

    gate_full, up_full, down_full = (
        lax.all_to_all(deliver(gate_rows), "expert", split_axis=0, concat_axis=0, tiled=True),
        lax.all_to_all(deliver(up_rows), "expert", split_axis=0, concat_axis=0, tiled=True),
        lax.all_to_all(deliver(down_rows), "expert", split_axis=0, concat_axis=0, tiled=True),
    )
    gate_full = gate_full.reshape(width, 2 * half)
    up_full = up_full.reshape(width, 2 * half)
    down_full = down_full.reshape(width, 2 * half)
    outputs = []
    marks = early_marks
    done = expert_rows(early_cells.reshape(-1, width), gate_full, up_full, down_full)
    done, marks = (done.reshape(early_cells.shape), marks)
    back = lax.all_to_all(done, "expert", split_axis=0, concat_axis=0, tiled=True)
    load = jnp.sum(marks)
    for batch in range(batches):
        outputs.append(
            combine(back[:, batch * CAP : (batch + 1) * CAP], routed[batch][2], pick_weight[batch])
        )
    return (jnp.stack(outputs, axis=0), load.astype(jnp.int32).reshape(1))


def solution(mesh):
    return jax.shard_map(
        per_device,
        mesh=mesh,
        in_specs=(
            P(None, ("groups", "expert"), None),
            P(None, ("groups", "expert"), None),
            P(None, ("groups", "expert"), None),
            P(None, ("groups", "expert"), None),
            P(),
            P("groups"),
            P("expert", None, None),
            P("expert", None, None),
            P("expert", None, None),
        ),
        out_specs=(P(None, ("groups", "expert"), None), P(("groups", "expert"))),
        check_vma=False,
    )
```

profile of v0, /device:TPU:0, one launch (start us, length us, event | category | flops | bytes accessed | tf_op | source)
XLA Modules:
  0.0 406.9 jit_solution(18082761906989629838)
XLA Ops:
  0.6 43.5 %all_to_all.49 = bf16[16,128,384]{2,1,0:T(8,128)(2,1)S(1)} all-to-all(bf16[16,128,384]{2,1,0:T(8,128)(2,1)} %bitcast.90), channel_id=1, replica_groups=mesh['groups'=2,'expert'=16] {'expert'}, dimensions={0} | all-to-all | bytes 3145728 | tf_op jit(solution)/shard_map/all_to_all | solution.py:90
  44.1 5.2 %all-to-all-start.5 = ((bf16[16,128,384]{2,1,0:T(8,128)(2,1)}), bf16[16,128,384]{2,1,0:T(8,128)(2,1)S(1)}, u32[]{:S(2)}, u32[]{:S(2)}) async-start(bf16[16,128,384]{2,1,0:T(8,128)(2,1)} %bitcast.91), calls=%async_computation.5 | async-start | bytes 3145728 | tf_op jit(solution)/shard_map/all_to_all | solution.py:93
  49.3 0.2 convert_reduce_fusion.2
  49.5 0.1 fusion.30
  49.6 0.2 select_reduce_fusion.5
  49.8 0.6 fusion.33
  50.4 0.1 convert_reduce_fusion.1
  50.5 0.5 fusion.34
  51.1 0.6 convert_reduce_fusion
  51.7 29.6 %all-to-all-done.5 = bf16[16,128,384]{2,1,0:T(8,128)(2,1)S(1)} async-done(((bf16[16,128,384]{2,1,0:T(8,128)(2,1)}), bf16[16,128,384]{2,1,0:T(8,128)(2,1)S(1)}, u32[]{:S(2)}, u32[]{:S(2)}) %all-to-all-start.5) | async-done | bytes 1572896 | tf_op jit(solution)/shard_map/all_to_all | solution.py:93
  81.2 9.3 %all-to-all-start.1 = ((bf16[16,128,384]{2,1,0:T(8,128)(2,1)}), bf16[16,128,384]{2,1,0:T(8,128)(2,1)}, u32[]{:S(2)}, u32[]{:S(2)}) async-start(bf16[16,128,384]{2,1,0:T(8,128)(2,1)} %bitcast.92), calls=%async_computation.1 | async-start | bytes 3145728 | tf_op jit(solution)/shard_map/all_to_all | solution.py:83
  90.5 0.1 reduce_sum.125
  90.6 0.1 reduce_sum.119
  90.7 0.7 gather_fusion
  91.4 0.1 gather.20
  91.5 0.7 fusion.32
  92.2 0.6 gather_fusion.1
  92.8 0.8 gather.22
  93.6 0.8 select_reduce_fusion.6
  94.3 0.6 compare_and_fusion.3
  95.0 0.2 broadcast_select_fusion.1
  95.1 1.1 broadcast_select_fusion
  96.2 1.0 pad_maximum_fusion.3
  97.2 1.9 gather_fusion.9
  99.1 1.9 gather_fusion.8
  101.1 1.9 gather_fusion.7
  103.0 1.9 gather_fusion.6
  104.9 17.7 %all-to-all-done.1 = bf16[16,128,384]{2,1,0:T(8,128)(2,1)} async-done(((bf16[16,128,384]{2,1,0:T(8,128)(2,1)}), bf16[16,128,384]{2,1,0:T(8,128)(2,1)}, u32[]{:S(2)}, u32[]{:S(2)}) %all-to-all-start.1) | async-done | bytes 1572896 | tf_op jit(solution)/shard_map/all_to_all | solution.py:83
  122.6 9.1 %all-to-all-start = ((bf16[16,4,2048]{2,1,0:T(4,128)(2,1)}), bf16[16,4,2048]{2,1,0:T(4,128)(2,1)S(1)}, u32[]{:S(2)}, u32[]{:S(2)}) async-start(bf16[16,4,2048]{2,1,0:T(4,128)(2,1)} %pad_maximum_fusion.3), calls=%async_computation | async-start | bytes 524288 | tf_op jit(solution)/shard_map/all_to_all | solution.py:79
  131.7 3.5 gather_fusion.4
  135.2 3.6 gather_fusion.5
  138.8 4.9 %select_bitcast_fusion.4 = (bf16[16,128,1,384]{3,1,0,2:T(8,128)(2,1)S(1)}, bf16[16,128,1,384]{3,1,0,2:T(8,128)(2,1)}, bf16[16,128,1,384]{3,1,0,2:T(8,128)(2,1)},...) fusion(bf16[16,128,384]{2,1,0:T(8,128)(2,1)} %gather_fusion.5, ...), kind=kLoop, calls=%fused_computation.27 | loop fusion | flops 4718592 | bytes 18874400 | tf_op jit(solution)/shard_map/stack | solution.py:109
  143.7 0.4 pad_maximum_fusion
  144.0 2.2 copy.26
  146.2 6.0 %all-to-all-start.2 = ((bf16[16,128,2,384]{3,1,2,0:T(8,128)(2,1)}), bf16[16,128,2,384]{3,1,2,0:T(8,128)(2,1)S(1)}, u32[]{:S(2)}, u32[]{:S(2)}) async-start(bf16[16,128,2,384]{3,1,2,0:T(8,128)(2,1)} %copy.26), calls=%async_computation.2 | async-start | bytes 6291456 | tf_op jit(solution)/shard_map/all_to_all | solution.py:114
  152.2 2.2 pad_maximum_fusion.1
  154.4 2.2 copy.28
  156.6 55.0 %all-to-all-done.2 = bf16[16,128,2,384]{3,1,2,0:T(8,128)(2,1)S(1)} async-done(((bf16[16,128,2,384]{3,1,2,0:T(8,128)(2,1)}), bf16[16,128,2,384]{3,1,2,0:T(8,128)(2,1)S(1)}, u32[]{:S(2)}, u32[]{:S(2)}) %all-to-all-start.2) | async-done | bytes 3145760 | tf_op jit(solution)/shard_map/all_to_all | solution.py:114
  211.6 15.5 %all-to-all-start.4 = ((bf16[16,128,2,384]{3,1,2,0:T(8,128)(2,1)}), bf16[16,128,2,384]{3,1,2,0:T(8,128)(2,1)}, u32[]{:S(2)}, u32[]{:S(2)}) async-start(bf16[16,128,2,384]{3,1,2,0:T(8,128)(2,1)} %copy.28), calls=%async_computation.4 | async-start | bytes 6291456 | tf_op jit(solution)/shard_map/all_to_all | solution.py:115
  227.0 2.2 pad_maximum_fusion.2
  229.3 2.2 copy.30
  231.5 55.0 %all-to-all-done.4 = bf16[16,128,2,384]{3,1,2,0:T(8,128)(2,1)} async-done(((bf16[16,128,2,384]{3,1,2,0:T(8,128)(2,1)}), bf16[16,128,2,384]{3,1,2,0:T(8,128)(2,1)}, u32[]{:S(2)}, u32[]{:S(2)}) %all-to-all-start.4) | async-done | bytes 3145760 | tf_op jit(solution)/shard_map/all_to_all | solution.py:115
  286.5 15.5 %all-to-all-start.6 = ((bf16[16,128,2,384]{3,1,2,0:T(8,128)(2,1)}), bf16[16,128,2,384]{3,1,2,0:T(8,128)(2,1)}, u32[]{:S(2)}, u32[]{:S(2)}) async-start(bf16[16,128,2,384]{3,1,2,0:T(8,128)(2,1)} %copy.30), calls=%async_computation.6 | async-start | bytes 6291456 | tf_op jit(solution)/shard_map/all_to_all | solution.py:116
  302.0 0.1 copy.33
  302.0 0.1 copy.32
  302.1 0.7 copy.34
  302.8 0.8 reshape.271
  303.6 3.5 copy.27
  307.1 4.1 %copy.29 = bf16[16,128,2,384]{1,0,3,2:T(8,128)(2,1)S(1)} copy(bf16[16,128,2,384]{3,1,2,0:T(8,128)(2,1)} %all-to-all-done.4) | data formatting | bytes 6291456 | tf_op jit(solution)/shard_map/all_to_all | solution.py:115
  311.3 3.7 fusion.6
  314.9 46.4 %all-to-all-done.6 = bf16[16,128,2,384]{3,1,2,0:T(8,128)(2,1)} async-done(((bf16[16,128,2,384]{3,1,2,0:T(8,128)(2,1)}), bf16[16,128,2,384]{3,1,2,0:T(8,128)(2,1)}, u32[]{:S(2)}, u32[]{:S(2)}) %all-to-all-start.6) | async-done | bytes 3145760 | tf_op jit(solution)/shard_map/all_to_all | solution.py:116
  361.4 15.4 %all-to-all-start.8 = ((s32[16,1,4]{2,1,0:T(1,128)}), s32[16,1,4]{2,1,0:T(1,128)S(1)}, u32[]{:S(2)}, u32[]{:S(2)}) async-start(s32[16,1,4]{2,1,0:T(1,128)} %copy.34), calls=%async_computation.8 | async-start | bytes 16384 | tf_op jit(solution)/shard_map/all_to_all | solution.py:80
  376.8 5.1 %copy.31 = bf16[16,128,2,384]{1,0,3,2:T(8,128)(2,1)} copy(bf16[16,128,2,384]{3,1,2,0:T(8,128)(2,1)} %all-to-all-done.6) | data formatting | bytes 6291456 | tf_op jit(solution)/shard_map/all_to_all | solution.py:116
  381.9 4.8 %fusion.9 = bf16[64,2048]{1,0:T(8,128)(2,1)} fusion(bf16[96,8,16,128]{3,2,1,0:T(8,128)(2,1)} %bitcast.88, bf16[64,2048]{1,0:T(8,128)(2,1)S(1)} %copy-done.2, bf16[96,8,16,128]{3,2,1,0:T(8,128)(2,1)S(1)} %bitcast.87, f32[64,768]{1,0:T(8,128)} %fusion.6), kind=kOutput, calls=%fused_computation.22 | convolution fusion | flops 403079168 | bytes 7012352 | tf_op jit(solution)/shard_map/dot_general | solution.py:21
  386.8 1.7 reshape.278
  388.5 6.0 %all-to-all-start.7 = ((bf16[16,4,2048]{2,1,0:T(4,128)(2,1)}), bf16[16,4,2048]{2,1,0:T(4,128)(2,1)S(1)}, u32[]{:S(2)}, u32[]{:S(2)}) async-start(bf16[16,4,2048]{2,1,0:T(4,128)(2,1)} %reshape.278), calls=%async_computation.7 | async-start | bytes 524288 | tf_op jit(solution)/shard_map/all_to_all | solution.py:125
  394.6 0.7 reduce_sum.129
  395.2 9.3 %all-to-all-done.7 = bf16[16,4,2048]{2,1,0:T(4,128)(2,1)S(1)} async-done(((bf16[16,4,2048]{2,1,0:T(4,128)(2,1)}), bf16[16,4,2048]{2,1,0:T(4,128)(2,1)S(1)}, u32[]{:S(2)}, u32[]{:S(2)}) %all-to-all-start.7) | async-done | bytes 262176 | tf_op jit(solution)/shard_map/all_to_all | solution.py:125
  404.6 0.2 fusion.36
  404.9 0.6 gather_fusion.2
  405.5 0.1 fusion.26
  405.6 0.6 gather_fusion.3
  406.2 0.1 fusion.25
  406.2 0.7 pad_maximum_fusion.4
  (47 shorter events, 0.3 us)
Async XLA Ops:
  44.1 5.2 %copy-start.8 = (s32[16]{0:T(128)S(1)}, s32[16]{0:T(128)}, u32[]{:S(2)}) copy-start(s32[16]{0:T(128)} %param.16) | copy-start | bytes 196
  44.1 5.4 %copy-start.12 = (s32[2,16,1]{1,2,0:T(1,128)S(1)}, s32[2,16,1]{1,2,0:T(1,128)}, u32[]{:S(2)}) copy-start(s32[2,16,1]{1,2,0:T(1,128)} %param.14) | copy-start | bytes 388
  44.1 5.4 %copy-start.13 = (s32[2,16,1]{1,2,0:T(1,128)S(1)}, s32[2,16,1]{1,2,0:T(1,128)}, u32[]{:S(2)}) copy-start(s32[2,16,1]{1,2,0:T(1,128)} %param.13) | copy-start | bytes 388
  44.1 37.1 %all-to-all-start.5 = ((bf16[16,128,384]{2,1,0:T(8,128)(2,1)}), bf16[16,128,384]{2,1,0:T(8,128)(2,1)S(1)}, u32[]{:S(2)}, u32[]{:S(2)}) async-start(bf16[16,128,384]{2,1,0:T(8,128)(2,1)} %bitcast.91), calls=%async_computation.5 | async-start | bytes 3145728 | tf_op jit(solution)/shard_map/all_to_all | solution.py:93
  81.2 9.5 %copy-start.3 = (bf16[2,16,2048]{2,1,0:T(8,128)(2,1)S(1)}, bf16[2,16,2048]{2,1,0:T(8,128)(2,1)}, u32[]{:S(2)}) copy-start(bf16[2,16,2048]{2,1,0:T(8,128)(2,1)} %param.11) | copy-start | bytes 393220
  81.2 41.3 %all-to-all-start.1 = ((bf16[16,128,384]{2,1,0:T(8,128)(2,1)}), bf16[16,128,384]{2,1,0:T(8,128)(2,1)}, u32[]{:S(2)}, u32[]{:S(2)}) async-start(bf16[16,128,384]{2,1,0:T(8,128)(2,1)} %bitcast.92), calls=%async_computation.1 | async-start | bytes 3145728 | tf_op jit(solution)/shard_map/all_to_all | solution.py:83
  94.9 8.1 %copy-start.5 = (s32[1024]{0:T(1024)}, s32[1024]{0:T(1024)S(1)}, u32[]{:S(2)}) copy-start(s32[1024]{0:T(1024)S(1)} %pad_clamp_fusion.3) | copy-start | bytes 12292
  94.9 6.1 %copy-start.4 = (s32[1024]{0:T(1024)}, s32[1024]{0:T(1024)S(1)}, u32[]{:S(2)}) copy-start(s32[1024]{0:T(1024)S(1)} %pad_clamp_fusion.2) | copy-start | bytes 12292
  122.6 23.6 %all-to-all-start = ((bf16[16,4,2048]{2,1,0:T(4,128)(2,1)}), bf16[16,4,2048]{2,1,0:T(4,128)(2,1)S(1)}, u32[]{:S(2)}, u32[]{:S(2)}) async-start(bf16[16,4,2048]{2,1,0:T(4,128)(2,1)} %pad_maximum_fusion.3), calls=%async_computation | async-start | bytes 524288 | tf_op jit(solution)/shard_map/all_to_all | solution.py:79
  135.1 3.6 copy-start
  135.2 3.6 copy-start.1
  135.2 3.6 copy-start.6
  135.2 3.6 copy-start.7
  146.2 65.4 %all-to-all-start.2 = ((bf16[16,128,2,384]{3,1,2,0:T(8,128)(2,1)}), bf16[16,128,2,384]{3,1,2,0:T(8,128)(2,1)S(1)}, u32[]{:S(2)}, u32[]{:S(2)}) async-start(bf16[16,128,2,384]{3,1,2,0:T(8,128)(2,1)} %copy.26), calls=%async_computation.2 | async-start | bytes 6291456 | tf_op jit(solution)/shard_map/all_to_all | solution.py:114
  211.6 74.9 %all-to-all-start.4 = ((bf16[16,128,2,384]{3,1,2,0:T(8,128)(2,1)}), bf16[16,128,2,384]{3,1,2,0:T(8,128)(2,1)}, u32[]{:S(2)}, u32[]{:S(2)}) async-start(bf16[16,128,2,384]{3,1,2,0:T(8,128)(2,1)} %copy.28), calls=%async_computation.4 | async-start | bytes 6291456 | tf_op jit(solution)/shard_map/all_to_all | solution.py:115
  286.5 74.9 %all-to-all-start.6 = ((bf16[16,128,2,384]{3,1,2,0:T(8,128)(2,1)}), bf16[16,128,2,384]{3,1,2,0:T(8,128)(2,1)}, u32[]{:S(2)}, u32[]{:S(2)}) async-start(bf16[16,128,2,384]{3,1,2,0:T(8,128)(2,1)} %copy.30), calls=%async_computation.6 | async-start | bytes 6291456 | tf_op jit(solution)/shard_map/all_to_all | solution.py:116
  307.1 4.2 %copy-start.2 = (bf16[64,2048]{1,0:T(8,128)(2,1)S(1)}, bf16[64,2048]{1,0:T(8,128)(2,1)}, u32[]{:S(2)}) copy-start(bf16[64,2048]{1,0:T(8,128)(2,1)} %reshape.271) | copy-start | bytes 786436
  361.4 27.1 %all-to-all-start.8 = ((s32[16,1,4]{2,1,0:T(1,128)}), s32[16,1,4]{2,1,0:T(1,128)S(1)}, u32[]{:S(2)}, u32[]{:S(2)}) async-start(s32[16,1,4]{2,1,0:T(1,128)} %copy.34), calls=%async_computation.8 | async-start | bytes 16384 | tf_op jit(solution)/shard_map/all_to_all | solution.py:80
  381.9 12.6 %copy-start.10 = (s32[16]{0:T(128)S(1)}, s32[16]{0:T(128)}, u32[]{:S(2)}) copy-start(s32[16]{0:T(128)} %get-tuple-element.15) | copy-start | bytes 196
  381.9 12.6 %copy-start.9 = (s32[16]{0:T(128)S(1)}, s32[16]{0:T(128)}, u32[]{:S(2)}) copy-start(s32[16]{0:T(128)} %get-tuple-element.13) | copy-start | bytes 196
  381.9 12.6 %copy-start.11 = (f32[2,16,1]{1,2,0:T(1,128)S(1)}, f32[2,16,1]{1,2,0:T(1,128)}, u32[]{:S(2)}) copy-start(f32[2,16,1]{1,2,0:T(1,128)} %param.12) | copy-start | bytes 388
  388.5 16.1 %all-to-all-start.7 = ((bf16[16,4,2048]{2,1,0:T(4,128)(2,1)}), bf16[16,4,2048]{2,1,0:T(4,128)(2,1)S(1)}, u32[]{:S(2)}, u32[]{:S(2)}) async-start(bf16[16,4,2048]{2,1,0:T(4,128)(2,1)} %reshape.278), calls=%async_computation.7 | async-start | bytes 524288 | tf_op jit(solution)/shard_map/all_to_all | solution.py:125
where the time goes:
time: 408 us; the launch traced here: 407 us
  waiting for transfers between devices  213 us (52%)
  starting transfers between devices  81.9 us (20%)
  blocking collectives  43.5 us (11%)
  local copies, waits for them, and re-layouts  41.3 us (10%)
  other arithmetic  17.8 us (4%)
  matrix products  8.5 us (2%)
    all_to_all x1, waiting for transfers between devices, per_device(): lax.all_to_all(deliver(up_rows), 'expert', split_axis=0, concat_axis=0, t...  55 us
    all_to_all x1, waiting for transfers between devices, per_device(): lax.all_to_all(deliver(gate_rows), 'expert', split_axis=0, concat_axis=0,...  55 us
    all_to_all x1, waiting for transfers between devices, per_device(): lax.all_to_all(deliver(down_rows), 'expert', split_axis=0, concat_axis=0,...  46.4 us
    all_to_all x1, blocking collectives, per_device(): lax.all_to_all(up_panel.reshape(slots, block, half), 'expert', split_axis...  43.5 us
    all_to_all x1, waiting for transfers between devices, per_device(): lax.all_to_all(down_panel.reshape(slots, block, half), 'expert', split_ax...  29.6 us
    all_to_all x1, waiting for transfers between devices, per_device(): lax.all_to_all(gate_panel.reshape(slots, block, half), 'expert', split_ax...  17.7 us
    all_to_all x1, starting transfers between devices, per_device(): lax.all_to_all(deliver(down_rows), 'expert', split_axis=0, concat_axis=0,...  15.5 us
    all_to_all x1, starting transfers between devices, per_device(): lax.all_to_all(deliver(up_rows), 'expert', split_axis=0, concat_axis=0, t...  15.5 us
  transfers between devices with their start and end apart: 8, of which 6 were waited for; matrix products, arithmetic and copies ran while one was open for 16% of the time, Pallas kernels for 0%

commit v1 on v0

v1 whole, which is shorter than its diff:
```python
import functools
import math

import jax
import jax.numpy as jnp
from jax import lax
from jax.experimental import pallas as pl
from jax.experimental.pallas import tpu as pltpu
from jax.sharding import PartitionSpec as P

MESH = pl.DeviceIdType.MESH
LANES = 128
ROWS = 256


def grid_of(devices):
    chips = devices // 2
    lo = max(d for d in range(1, math.isqrt(chips) + 1) if chips % d == 0)
    return chips // lo, lo


def layer_kernel(
    n,
    hi,
    lo,
    act_ref,
    weight_ref,
    ids_ref,
    rep_ref,
    home_ref,
    row_ref,
    col_ref,
    gate_ref,
    up_ref,
    down_ref,
    out_ref,
    load_ref,
    tok,
    wgu,
    wd,
    hid,
    res,
    xbuf,
    comb,
    fin,
    local_sem,
    wd_sem,
    z_send,
    z_recv,
    x_send,
    x_recv,
    s_send,
    s_recv,
    h_send,
    h_recv,
    rx_send,
    rx_recv,
    rz_send,
    rz_recv,
):
    batches, t, width = act_ref.shape
    top = ids_ref.shape[2]
    half = gate_ref.shape[2]
    wide = width // 2
    me = lax.axis_index("expert")
    core = lax.rem(me, 2)
    chip = me // 2
    xi = lax.rem(chip, lo)
    zi = chip // lo

    def index(dz, dx, dc):
        z = lax.rem(zi + dz + hi, hi)
        x = lax.rem(xi + dx + lo, lo)
        c = lax.rem(core + dc, 2)
        return (z * lo + x) * 2 + c

    def rows(device, count=1):
        return pl.ds(pl.multiple_of(device * t, t), count * t)

    def remote(src, dst, send, recv, device):
        copy = pltpu.make_async_remote_copy(
            src_ref=src,
            dst_ref=dst,
            send_sem=send,
            recv_sem=recv,
            device_id={"expert": device},
            device_id_type=MESH,
        )
        copy.start()
        return copy

    def local(src, dst, sem):
        copy = pltpu.make_async_copy(src, dst, sem)
        copy.start()
        return copy

    own_cols = pl.ds(pl.multiple_of(core * half, LANES), half)
    act_copies = [
        local(act_ref.at[g], tok.at[g, rows(me), pl.ds(0, width)], local_sem.at[g])
        for g in range(batches)
    ]
    gate_copy = local(gate_ref.at[0], wgu.at[:, pl.ds(0, half)], local_sem.at[batches])
    up_copy = local(up_ref.at[0], wgu.at[:, pl.ds(half, half)], local_sem.at[batches + 1])
    own_half = pl.ds(pl.multiple_of(core * wide, wide), wide)
    other_half = pl.ds(pl.multiple_of((1 - core) * wide, wide), wide)
    down_copy = local(down_ref.at[0, own_half], wd.at[:, own_cols], local_sem.at[batches + 2])

    peers = [index(dz, 0, dc) for dz in range(hi) for dc in range(2) if dz or dc]
    peers += [index(0, dx, 0) for dx in range(1, lo)]
    barrier = pltpu.get_barrier_semaphore()
    for peer in peers:
        pl.semaphore_signal(barrier, inc=1, device_id={"expert": peer}, device_id_type=MESH)

    row = row_ref[...]
    col = col_ref[...]
    slots = row.shape[1]
    s_lane = lax.broadcasted_iota(jnp.int32, (slots, slots), 1)
    s_row = lax.broadcasted_iota(jnp.int32, (slots, slots), 0)
    earlier = (col == row) & (s_row < s_lane)
    ranks = jnp.sum(earlier.astype(jnp.int32), axis=0, keepdims=True)
    homes = home_ref[...]
    lane_slot = lax.broadcasted_iota(jnp.int32, (t, slots), 1)
    lane_expert = lax.broadcasted_iota(jnp.int32, (t, homes.shape[1]), 1)
    lane = lax.broadcasted_iota(jnp.int32, (t, LANES), 1)
    for g in range(batches):
        marks = jnp.zeros((t, LANES), jnp.float32)
        for k in range(top):
            ids = ids_ref[g, :, k : k + 1]
            rep = rep_ref[g, :, k : k + 1]
            weight = weight_ref[g, :, k : k + 1]
            home = jnp.sum(jnp.where(lane_expert == ids, homes, 0), axis=1, keepdims=True)
            match = (row == ids) & (ranks == rep)
            slot = jnp.sum(jnp.where(match, lane_slot, 0), axis=1, keepdims=True)
            first = weight.astype(jnp.bfloat16).astype(jnp.float32)
            second = (weight - first).astype(jnp.bfloat16).astype(jnp.float32)
            third = weight - first - second
            parts = (home.astype(jnp.float32), slot.astype(jnp.float32), first, second, third)
            for place, part in enumerate(parts):
                marks = jnp.where(lane == place * top + k, part, marks)
        tok[g, rows(me), pl.ds(width, LANES)] = marks.astype(jnp.bfloat16)

    pl.semaphore_wait(barrier, len(peers))

    pending = []
    pending.append(
        remote(down_ref.at[0, other_half], wd.at[:, own_cols], wd_sem.at[0], wd_sem.at[1], index(0, 0, 1))
    )

    def forward(g, dz, dx):
        block = tok.at[g, rows(index(-dz, -dx, 0))]
        pending.append(
            remote(block, block, s_send.at[g, dz, dx], s_recv.at[g, dz, dx], index(0, 0, 1))
        )

    def across(g, dz):
        block = tok.at[g, rows(index(-dz, 0, 0))]
        for dx in range(1, lo):
            pending.append(
                remote(
                    block, block, x_send.at[g, dz, dx], x_recv.at[g, dz, dx], index(0, dx, 0)
                )
            )
        forward(g, dz, 0)

    def arrived(ref, send, recv):
        pltpu.make_async_remote_copy(
            src_ref=ref,
            dst_ref=ref,
            send_sem=send,
            recv_sem=recv,
            device_id={"expert": index(0, 0, 1)},
            device_id_type=MESH,
        ).wait_recv()

    def send_z(g):
        act_copies[g].wait()
        block = tok.at[g, rows(me)]
        for dz in range(1, hi):
            pending.append(
                remote(block, block, z_send.at[g, dz], z_recv.at[g, dz], index(dz, 0, 0))
            )
        across(g, 0)

    def relay_z(g):
        for dz in range(1, hi):
            arrived(tok.at[g, rows(index(-dz, 0, 0))], z_send.at[g, dz], z_recv.at[g, dz])
            across(g, dz)

    def relay_x(g):
        for dz in range(hi):
            for dx in range(1, lo):
                arrived(
                    tok.at[g, rows(index(-dz, -dx, 0))],
                    x_send.at[g, dz, dx],
                    x_recv.at[g, dz, dx],
                )
                forward(g, dz, dx)

    def await_all(g):
        for dz in range(hi):
            for dx in range(lo):
                arrived(
                    tok.at[g, rows(index(-dz, -dx, 1))],
                    s_send.at[g, dz, dx],
                    s_recv.at[g, dz, dx],
                )

    total = n * t
    step = min(ROWS, total)

    def chunks(body):
        if total == step:
            body(pl.ds(0, step))
        else:

            @pl.loop(0, total // step)
            def _(i):
                body(pl.ds(pl.multiple_of(i * step, step), step))

    def hidden(g):
        def body(part):
            both = jnp.dot(
                tok[g, part, pl.ds(0, width)], wgu[...], preferred_element_type=jnp.float32
            )
            gate, up = both[:, :half], both[:, half:]
            value = gate / (1.0 + jnp.exp(-gate)) * up
            hid[g, part, own_cols] = value.astype(jnp.bfloat16)

        chunks(body)
        mine = hid.at[g, :, own_cols]
        pending.append(remote(mine, mine, h_send.at[g], h_recv.at[g], index(0, 0, 1)))

    def result(g):
        other_cols = pl.ds(pl.multiple_of((1 - core) * half, LANES), half)
        arrived(hid.at[g, :, other_cols], h_send.at[g], h_recv.at[g])

        def body(part):
            value = lax.dot_general(
                hid[g, part, :],
                wd[...],
                (((1,), (1,)), ((), ())),
                preferred_element_type=jnp.float32,
            )
            value = value.astype(jnp.bfloat16).astype(jnp.float32)
            marks = tok[g, part, pl.ds(width, LANES)].astype(jnp.float32)
            scale = jnp.zeros((step, 1), jnp.float32)
            for k in range(top):
                home, _, first, second, third = (
                    marks[:, p * top + k : p * top + k + 1] for p in range(5)
                )
                weight = first + (second + third)
                scale += jnp.where(home == chip.astype(jnp.float32), weight, 0.0)
            res[g, part, :] = (value * scale).astype(jnp.bfloat16)

        chunks(body)
        for dz in list(range(1, hi)) + [0]:
            for dx in range(1, lo):
                pending.append(
                    remote(
                        res.at[g, rows(index(dz, dx, 0) - core, 2)],
                        xbuf.at[g, dx, dz],
                        rx_send.at[g, dz, dx],
                        rx_recv.at[g, dz, dx],
                        index(0, dx, 0),
                    )
                )

    def collect(g):
        for dz in list(range(1, hi)) + [0]:
            value = res[g, rows(index(dz, 0, 0) - core, 2), :].astype(jnp.float32)
            for dx in range(1, lo):
                arrived(xbuf.at[g, dx, dz], rx_send.at[g, dz, dx], rx_recv.at[g, dz, dx])
                value += xbuf[g, dx, dz].astype(jnp.float32)
            comb[g, dz] = value.astype(jnp.bfloat16)
            for dc in range(2):
                block = comb.at[g, dz, pl.ds(pl.multiple_of(lax.rem(core + dc, 2) * t, t), t)]
                if dz or dc:
                    pending.append(
                        remote(
                            block,
                            fin.at[g, dz, core],
                            rz_send.at[g, dz, dc],
                            rz_recv.at[g, dz, dc],
                            index(dz, 0, dc),
                        )
                    )
                else:
                    fin[g, dz, core] = block[...]

    def finish(g):
        for dz in range(hi):
            for dc in range(2):
                if dz or dc:
                    arrived(
                        fin.at[g, dz, lax.rem(core + dc, 2)],
                        rz_send.at[g, dz, dc],
                        rz_recv.at[g, dz, dc],
                    )
        for c in range(2):
            value = fin[g, 0, c].astype(jnp.float32)
            for dz in range(1, hi):
                value += fin[g, dz, c].astype(jnp.float32)
            out_ref[g, :, pl.ds(c * wide, wide)] = value.astype(jnp.bfloat16)

    send_z(0)
    relay_z(0)
    for g in range(1, batches):
        send_z(g)
    relay_x(0)
    gate_copy.wait()
    up_copy.wait()
    await_all(0)
    hidden(0)
    down_copy.wait()
    arrived(wd.at[:, own_cols], wd_sem.at[0], wd_sem.at[1])
    for g in range(batches):
        if g + 1 < batches:
            relay_z(g + 1)
        result(g)
        if g + 1 < batches:
            relay_x(g + 1)
            await_all(g + 1)
            hidden(g + 1)
        collect(g)

    count = jnp.zeros((1, 1), jnp.float32)
    for g in range(batches):
        marks = tok[g, :, pl.ds(width, LANES)].astype(jnp.float32)
        place = lax.broadcasted_iota(jnp.int32, marks.shape, 1)
        mine = (place >= top) & (place < 2 * top) & (marks == me.astype(jnp.float32))
        per_lane = jnp.sum(jnp.where(mine, 1.0, 0.0), axis=0, keepdims=True)
        count += jnp.sum(per_lane, axis=1, keepdims=True)
    load_ref[...] = count.astype(jnp.int32)

    for g in range(batches):
        finish(g)
    for copy in pending:
        copy.wait_send()


def per_device(
    activations,
    pick_weight,
    expert_ids,
    replica,
    old_home,
    new_expert,
    gate_panel,
    up_panel,
    down_panel,
):
    n = lax.axis_size("expert")
    hi, lo = grid_of(n)
    batches, t, width = activations.shape
    half = gate_panel.shape[2]
    wide = width // 2
    total = n * t
    dma = pltpu.SemaphoreType.DMA
    vmem = pl.BlockSpec(memory_space=pltpu.VMEM)
    hbm = pl.BlockSpec(memory_space=pl.ANY)
    bf16 = jnp.bfloat16
    out, load = pl.pallas_call(
        functools.partial(layer_kernel, n, hi, lo),
        out_shape=(
            jax.ShapeDtypeStruct(activations.shape, bf16),
            jax.ShapeDtypeStruct((1, 1), jnp.int32),
        ),
        in_specs=[hbm, vmem, vmem, vmem, vmem, vmem, vmem, hbm, hbm, hbm],
        out_specs=(vmem, vmem),
        scratch_shapes=[
            pltpu.VMEM((batches, total, width + LANES), bf16),
            pltpu.VMEM((width, 2 * half), bf16),
            pltpu.VMEM((wide, 2 * half), bf16),
            pltpu.VMEM((batches, total, 2 * half), bf16),
            pltpu.VMEM((batches, total, wide), bf16),
            pltpu.VMEM((batches, lo, hi, 2 * t, wide), bf16),
            pltpu.VMEM((batches, hi, 2 * t, wide), bf16),
            pltpu.VMEM((batches, hi, 2, t, wide), bf16),
            dma((batches + 3,)),
            dma((2,)),
            dma((batches, hi)),
            dma((batches, hi)),
            dma((batches, hi, lo)),
            dma((batches, hi, lo)),
            dma((batches, hi, lo)),
            dma((batches, hi, lo)),
            dma((batches,)),
            dma((batches,)),
            dma((batches, hi, lo)),
            dma((batches, hi, lo)),
            dma((batches, hi, 2)),
            dma((batches, hi, 2)),
        ],
        compiler_params=pltpu.CompilerParams(
            collective_id=0, has_side_effects=True, vmem_limit_bytes=60 * 1024 * 1024
        ),
        cost_estimate=pl.CostEstimate(
            flops=6 * batches * total * width * half,
            bytes_accessed=6 * width * half,
            transcendentals=batches * total * half,
        ),
        name="expert_layer",
    )(
        activations,
        pick_weight,
        expert_ids,
        replica,
        old_home.reshape(1, -1),
        new_expert.reshape(1, -1),
        new_expert.reshape(-1, 1),
        gate_panel,
        up_panel,
        down_panel,
    )
    return out, load.reshape(1)


def solution(mesh):
    return jax.shard_map(
        per_device,
        mesh=mesh,
        in_specs=(
            P(None, ("groups", "expert"), None),
            P(None, ("groups", "expert"), None),
            P(None, ("groups", "expert"), None),
            P(None, ("groups", "expert"), None),
            P(),
            P("groups"),
            P("expert", None, None),
            P("expert", None, None),
            P("expert", None, None),
        ),
        out_specs=(P(None, ("groups", "expert"), None), P(("groups", "expert"))),
        check_vma=False,
    )
```

time: 408 us -> 55.5 us (0.14)
  waiting for transfers between devices: 213 us -> 0 us
  starting transfers between devices: 81.9 us -> 0 us
  Pallas kernels: 0 us -> 45.8 us
  blocking collectives: 43.5 us -> 0 us
  local copies, waits for them, and re-layouts: 41.3 us -> 6.97 us
  other arithmetic: 17.8 us -> 0 us
  matrix products: 8.5 us -> 0 us
    all_to_all x8 -> x0, waiting for transfers between devices: 213 us -> none  [the longest x1 55 us: per_device(): lax.all_to_all(deliver(up_rows), 'expert', split_axis=0, concat_axis=0, t...]
    all_to_all x8 -> x0, starting transfers between devices: 81.9 us -> none  [the longest x1 15.5 us: per_device(): lax.all_to_all(deliver(down_rows), 'expert', split_axis=0, concat_axis=0,...]
    pallas_call x0 -> x1, Pallas kernels: none -> 45.8 us  [per_device(): pl.pallas_call(functools.partial(layer_kernel, n, hi, lo), out_shape=(jax...]
    all_to_all x1 -> x0, blocking collectives: 43.5 us -> none  [per_device(): lax.all_to_all(up_panel.reshape(slots, block, half), 'expert', split_axis...]
    gather x12 -> x0, local copies, waits for them, and re-layouts: 18.1 us -> none  [the longest x3 7.42 us: deliver(): jnp.take(pieces, second, axis=0)]
    all_to_all x4 -> x0, local copies, waits for them, and re-layouts: 13.5 us -> none  [the longest x1 5.1 us: per_device(): lax.all_to_all(deliver(down_rows), 'expert', split_axis=0, concat_axis=0,...]
    another operation x7 -> x0, other arithmetic: 10.4 us -> none  [the longest x4 9.71 us: deliver(): jnp.stack((jnp.take(pieces, first, axis=0), jnp.take(pieces, second, axis...]
    dot_general x2 -> x0, matrix products: 8.5 us -> none  [the longest x1 4.84 us: expert_rows(): lax.dot_general(hidden, down_full, (((1,), (1,)), ((), ())), preferred_el...]
  transfers between devices with their start and end apart: 8 -> 0, of which waited for: 6 -> 0; matrix products, arithmetic and copies ran while one was open for 16% -> 0% of each run, Pallas kernels for 0% -> 0%
where the time goes in v1:
time: 55.5 us; the launch traced here: 55.2 us
  Pallas kernels  45.8 us (83%)
  local copies, waits for them, and re-layouts  6.97 us (13%)
  between operations  2.39 us (4%)
    pallas_call x1, Pallas kernels, per_device(): pl.pallas_call(functools.partial(layer_kernel, n, hi, lo), out_shape=(jax...  45.8 us
    unnamed x4, local copies, waits for them, and re-layouts  5.65 us
    reshape x1, local copies, waits for them, and re-layouts, per_device(): new_expert.reshape(-1, 1)  1.32 us

profile of v1, /device:TPU:0, one launch (start us, length us, event | category | flops | bytes accessed | tf_op | source)
XLA Modules:
  0.0 55.2 jit_solution(14055983943659352282)
XLA Ops:
  0.6 1.3 %copy.14.col_ref = s32[16,1]{1,0:T(8,128)} copy(s32[16,1]{0,1:T(1,128)} %bitcast.4) | data formatting | bytes 128 | tf_op jit(solution)/shard_map/reshape | solution.py:410
  2.0 1.4 %copy.11.weight_ref = f32[2,16,1]{2,1,0:T(8,128)} copy(f32[2,16,1]{1,2,0:T(1,128)} %param.10) | data formatting | bytes 256 | tf_op args[1]
  3.3 1.4 %copy.12.ids_ref = s32[2,16,1]{2,1,0:T(8,128)} copy(s32[2,16,1]{1,2,0:T(1,128)} %param.11) | data formatting | bytes 256 | tf_op args[2]
  4.7 1.4 %copy.13.rep_ref = s32[2,16,1]{2,1,0:T(8,128)} copy(s32[2,16,1]{1,2,0:T(1,128)} %param.12) | data formatting | bytes 256 | tf_op args[3]
  6.0 45.8 %expert_layer.1 = (bf16[2,16,2048]{2,1,0:T(8,128)(2,1)}, s32[1,1]{1,0:T(1,128)}) custom-call(bf16[2,16,2048]{2,1,0:T(8,128)(2,1)} %act_ref.1, f32[2,16,1]{2,1,0:T(8,128)} %copy.11.weight_ref, s32[2,16,1]{2,1,0:T(8,128)} %copy.12.ids_ref, s32[2,16,1]{2,1,0:T(8,128)} %copy.13.rep_ref, s32[1,8]{1,0:T(1,128)} %bitcast.6, s32[1,16]{1,0:T(1,128)} %bitcast.5, ...), custom_call_target="tpu_custom_call" | custom-call | flops 2415919104 | bytes 4718592 | tf_op jit(solution)/shard_map/expert_layer/pallas_call | solution.py:362
  51.8 1.6 %copy.17 = bf16[2,16,2048]{2,1,0:T(8,128)(2,1)} copy(bf16[2,16,2048]{2,1,0:T(8,128)(2,1)} %get-tuple-element.8) | data formatting | bytes 262144

commit v2 on v1

v2 whole, which is shorter than its diff:
```python
import functools
import math

import jax
import jax.numpy as jnp
from jax import lax
from jax.experimental import pallas as pl
from jax.experimental.pallas import tpu as pltpu
from jax.sharding import PartitionSpec as P

MESH = pl.DeviceIdType.MESH
LANES = 128
ROWS = 256


def grid_of(devices):
    chips = devices // 2
    lo = max(d for d in range(1, math.isqrt(chips) + 1) if chips % d == 0)
    return chips // lo, lo


def layer_kernel(
    hi,
    lo,
    act_ref,
    weight_ref,
    ids_ref,
    rep_ref,
    home_ref,
    row_ref,
    gate_ref,
    up_ref,
    down_ref,
    out_ref,
    load_ref,
    tok,
    wgu,
    wd,
    res,
    xbuf,
    comb,
    fin,
    tally,
    local_sem,
    panel_send,
    panel_recv,
    z_send,
    z_recv,
    x_send,
    x_recv,
    rx_send,
    rx_recv,
    rz_send,
    rz_recv,
    tally_sem,
):
    batches, t, width = act_ref.shape
    top = ids_ref.shape[1]
    half = gate_ref.shape[2]
    full = 2 * half
    me = lax.axis_index("expert")
    core = lax.rem(me, 2)
    chip = me // 2
    xi = lax.rem(chip, lo)
    zi = chip // lo
    sibling = chip * 2 + (1 - core)

    def chip_at(dz, dx):
        z = lax.rem(zi + dz + hi, hi)
        x = lax.rem(xi + dx + lo, lo)
        return z * lo + x

    def device_at(dz, dx):
        return chip_at(dz, dx) * 2 + core

    def rows(place):
        return pl.ds(pl.multiple_of(place * t, t), t)

    def remote(src, dst, send, recv, device):
        copy = pltpu.make_async_remote_copy(
            src_ref=src,
            dst_ref=dst,
            send_sem=send,
            recv_sem=recv,
            device_id={"expert": device},
            device_id_type=MESH,
        )
        copy.start()
        return copy

    def arrived(ref, send, recv):
        pltpu.make_async_remote_copy(
            src_ref=ref,
            dst_ref=ref,
            send_sem=send,
            recv_sem=recv,
            device_id={"expert": sibling},
            device_id_type=MESH,
        ).wait_recv()

    def local(src, dst, sem):
        copy = pltpu.make_async_copy(src, dst, sem)
        copy.start()
        return copy

    peers = [device_at(dz, 0) for dz in range(1, hi)]
    peers += [device_at(0, dx) for dx in range(1, lo)] + [sibling]
    barrier = pltpu.get_barrier_semaphore()
    for peer in peers:
        pl.semaphore_signal(barrier, inc=1, device_id={"expert": peer}, device_id_type=MESH)

    gate_cols = pl.ds(pl.multiple_of(core * half, LANES), half)
    up_cols = pl.ds(pl.multiple_of(full + core * half, LANES), half)
    panels = (
        (gate_ref.at[0], wgu.at[:, gate_cols]),
        (up_ref.at[0], wgu.at[:, up_cols]),
        (down_ref.at[0], wd.at[:, gate_cols]),
    )
    act_copies = [
        local(act_ref.at[g], tok.at[g, rows(chip), pl.ds(0, width)], local_sem.at[g])
        for g in range(batches)
    ]
    panel_copies = [
        local(src, dst, local_sem.at[batches + p]) for p, (src, dst) in enumerate(panels)
    ]

    def upright(line):
        count = line.shape[1]
        shape = (count, count)
        same = lax.broadcasted_iota(jnp.int32, shape, 0) == lax.broadcasted_iota(
            jnp.int32, shape, 1
        )
        return jnp.sum(jnp.where(same, line, jnp.zeros_like(line)), axis=1, keepdims=True)

    row = row_ref[...]
    slots = row.shape[1]
    s_lane = lax.broadcasted_iota(jnp.int32, (slots, slots), 1)
    s_row = lax.broadcasted_iota(jnp.int32, (slots, slots), 0)
    earlier = (upright(row) == row) & (s_row < s_lane)
    ranks = jnp.sum(earlier.astype(jnp.int32), axis=0, keepdims=True)
    homes = home_ref[...]
    lane_slot = lax.broadcasted_iota(jnp.int32, (t, slots), 1)
    lane_expert = lax.broadcasted_iota(jnp.int32, (t, homes.shape[1]), 1)
    lane = lax.broadcasted_iota(jnp.int32, (t, LANES), 1)
    for g in range(batches):
        marks = jnp.zeros((t, LANES), jnp.float32)
        for k in range(top):
            ids = upright(ids_ref[g, k : k + 1, :])
            rep = upright(rep_ref[g, k : k + 1, :])
            weight = upright(weight_ref[g, k : k + 1, :])
            home = jnp.sum(jnp.where(lane_expert == ids, homes, 0), axis=1, keepdims=True)
            match = (row == ids) & (ranks == rep)
            slot = jnp.sum(jnp.where(match, lane_slot, 0), axis=1, keepdims=True)
            first = weight.astype(jnp.bfloat16).astype(jnp.float32)
            second = (weight - first).astype(jnp.bfloat16).astype(jnp.float32)
            third = weight - first - second
            parts = (home.astype(jnp.float32), slot.astype(jnp.float32), first, second, third)
            for place, part in enumerate(parts):
                marks = jnp.where(lane == place * top + k, part, marks)
        tok[g, rows(chip), pl.ds(width, LANES)] = marks.astype(jnp.bfloat16)

    pl.semaphore_wait(barrier, len(peers))

    pending = []

    def across(g, dz):
        block = tok.at[g, rows(chip_at(-dz, 0))]
        for dx in range(1, lo):
            pending.append(
                remote(
                    block, block, x_send.at[g, dz, dx], x_recv.at[g, dz, dx], device_at(0, dx)
                )
            )

    def send_z(g):
        act_copies[g].wait()
        block = tok.at[g, rows(chip)]
        for dz in range(1, hi):
            pending.append(
                remote(block, block, z_send.at[g, dz], z_recv.at[g, dz], device_at(dz, 0))
            )
        across(g, 0)

    def relay_z(g):
        for dz in range(1, hi):
            arrived(tok.at[g, rows(chip_at(-dz, 0))], z_send.at[g, dz], z_recv.at[g, dz])
            across(g, dz)

    def await_x(g):
        for dz in range(hi):
            for dx in range(1, lo):
                arrived(
                    tok.at[g, rows(chip_at(-dz, -dx))],
                    x_send.at[g, dz, dx],
                    x_recv.at[g, dz, dx],
                )

    total = hi * lo * t
    step = min(ROWS, total)

    def expert(g):
        def body(part):
            both = jnp.dot(
                tok[g, part, pl.ds(0, width)], wgu[...], preferred_element_type=jnp.float32
            )
            gate, up = both[:, :full], both[:, full:]
            hidden = (gate / (1.0 + jnp.exp(-gate)) * up).astype(jnp.bfloat16)
            value = lax.dot_general(
                hidden, wd[...], (((1,), (1,)), ((), ())), preferred_element_type=jnp.float32
            )
            value = value.astype(jnp.bfloat16).astype(jnp.float32)
            marks = tok[g, part, pl.ds(width, LANES)].astype(jnp.float32)
            scale = jnp.zeros((step, 1), jnp.float32)
            for k in range(top):
                home, _, first, second, third = (
                    marks[:, p * top + k : p * top + k + 1] for p in range(5)
                )
                weight = first + (second + third)
                scale += jnp.where(home == chip.astype(jnp.float32), weight, 0.0)
            res[g, part, :] = (value * scale).astype(jnp.bfloat16)

        if total == step:
            body(pl.ds(0, step))
        else:

            @pl.loop(0, total // step)
            def _(i):
                body(pl.ds(pl.multiple_of(i * step, step), step))

        for dz in back_order:
            for dx in range(1, lo):
                pending.append(
                    remote(
                        res.at[g, rows(chip_at(dz, dx))],
                        xbuf.at[g, dx, dz],
                        rx_send.at[g, dz, dx],
                        rx_recv.at[g, dz, dx],
                        device_at(0, dx),
                    )
                )

    back_order = list(range(1, hi)) + [0]

    def collect(g):
        for dz in back_order:
            value = res[g, rows(chip_at(dz, 0)), :].astype(jnp.float32)
            for dx in range(1, lo):
                arrived(xbuf.at[g, dx, dz], rx_send.at[g, dz, dx], rx_recv.at[g, dz, dx])
                value += xbuf[g, dx, dz].astype(jnp.float32)
            if dz:
                comb[g, dz] = value.astype(jnp.bfloat16)
                pending.append(
                    remote(
                        comb.at[g, dz],
                        fin.at[g, dz],
                        rz_send.at[g, dz],
                        rz_recv.at[g, dz],
                        device_at(dz, 0),
                    )
                )
            else:
                fin[g, 0] = value.astype(jnp.bfloat16)

    def finish(g):
        value = fin[g, 0].astype(jnp.float32)
        for dz in range(1, hi):
            arrived(fin.at[g, dz], rz_send.at[g, dz], rz_recv.at[g, dz])
            value += fin[g, dz].astype(jnp.float32)
        out_ref[g] = value.astype(jnp.bfloat16)

    def picks_of(slot):
        count = jnp.zeros((1, 1), jnp.float32)
        for g in range(batches):
            marks = tok[g, :, pl.ds(width, LANES)].astype(jnp.float32)
            place = lax.broadcasted_iota(jnp.int32, marks.shape, 1)
            mine = (place >= top) & (place < 2 * top) & (marks == slot.astype(jnp.float32))
            per_lane = jnp.sum(jnp.where(mine, 1.0, 0.0), axis=0, keepdims=True)
            count += jnp.sum(per_lane, axis=1, keepdims=True)
        return count

    send_z(0)
    pushed = [
        remote(src, dst, panel_send.at[p], panel_recv.at[p], sibling)
        for p, (src, dst) in enumerate(panels)
    ]
    pending.extend(pushed)
    relay_z(0)
    for g in range(1, batches):
        send_z(g)
    await_x(0)
    for p, (copy, (_, dst)) in enumerate(zip(panel_copies, panels)):
        copy.wait()
        other_cols = (
            wgu.at[:, pl.ds(pl.multiple_of((1 - core) * half, LANES), half)],
            wgu.at[:, pl.ds(pl.multiple_of(full + (1 - core) * half, LANES), half)],
            wd.at[:, pl.ds(pl.multiple_of((1 - core) * half, LANES), half)],
        )[p]
        arrived(other_cols, panel_send.at[p], panel_recv.at[p])
    for g in range(batches):
        if g + 1 < batches:
            relay_z(g + 1)
        expert(g)
        if g + 1 < batches:
            await_x(g + 1)
        collect(g)

    tally[0] = jnp.broadcast_to(picks_of(sibling), tally.shape[1:])
    swap = remote(tally.at[0], tally.at[1], tally_sem.at[0], tally_sem.at[1], sibling)
    pending.append(swap)
    count = picks_of(me)
    for g in range(batches):
        finish(g)
    arrived(tally.at[1], tally_sem.at[0], tally_sem.at[1])
    load_ref[...] = (count + tally[1, :1, :1]).astype(jnp.int32)
    for copy in pending:
        copy.wait_send()


def per_device(
    activations,
    pick_weight,
    expert_ids,
    replica,
    old_home,
    new_expert,
    gate_panel,
    up_panel,
    down_panel,
):
    n = lax.axis_size("expert")
    hi, lo = grid_of(n)
    batches, t, width = activations.shape
    half = gate_panel.shape[2]
    total = hi * lo * t
    dma = pltpu.SemaphoreType.DMA
    vmem = pl.BlockSpec(memory_space=pltpu.VMEM)
    hbm = pl.BlockSpec(memory_space=pl.ANY)
    bf16 = jnp.bfloat16
    out, load = pl.pallas_call(
        functools.partial(layer_kernel, hi, lo),
        out_shape=(
            jax.ShapeDtypeStruct(activations.shape, bf16),
            jax.ShapeDtypeStruct((1, 1), jnp.int32),
        ),
        in_specs=[hbm, vmem, vmem, vmem, vmem, vmem, hbm, hbm, hbm],
        out_specs=(vmem, vmem),
        scratch_shapes=[
            pltpu.VMEM((batches, total, width + LANES), bf16),
            pltpu.VMEM((width, 4 * half), bf16),
            pltpu.VMEM((width, 2 * half), bf16),
            pltpu.VMEM((batches, total, width), bf16),
            pltpu.VMEM((batches, lo, hi, t, width), bf16),
            pltpu.VMEM((batches, hi, t, width), bf16),
            pltpu.VMEM((batches, hi, t, width), bf16),
            pltpu.VMEM((2, 8, LANES), jnp.float32),
            dma((batches + 3,)),
            dma((3,)),
            dma((3,)),
            dma((batches, hi)),
            dma((batches, hi)),
            dma((batches, hi, lo)),
            dma((batches, hi, lo)),
            dma((batches, hi, lo)),
            dma((batches, hi, lo)),
            dma((batches, hi)),
            dma((batches, hi)),
            dma((2,)),
        ],
        compiler_params=pltpu.CompilerParams(
            collective_id=0, has_side_effects=True, vmem_limit_bytes=60 * 1024 * 1024
        ),
        cost_estimate=pl.CostEstimate(
            flops=12 * batches * total * width * half,
            bytes_accessed=12 * width * half,
            transcendentals=2 * batches * total * half,
        ),
        name="expert_layer",
    )(
        activations,
        pick_weight.transpose(0, 2, 1),
        expert_ids.transpose(0, 2, 1),
        replica.transpose(0, 2, 1),
        old_home.reshape(1, -1),
        new_expert.reshape(1, -1),
        gate_panel,
        up_panel,
        down_panel,
    )
    return out, load.reshape(1)


def solution(mesh):
    return jax.shard_map(
        per_device,
        mesh=mesh,
        in_specs=(
            P(None, ("groups", "expert"), None),
            P(None, ("groups", "expert"), None),
            P(None, ("groups", "expert"), None),
            P(None, ("groups", "expert"), None),
            P(),
            P("groups"),
            P("expert", None, None),
            P("expert", None, None),
            P("expert", None, None),
        ),
        out_specs=(P(None, ("groups", "expert"), None), P(("groups", "expert"))),
        check_vma=False,
    )
```

time: 55.5 us -> 46.3 us (0.83)
  local copies, waits for them, and re-layouts: 6.97 us -> 1.57 us
  Pallas kernels: 45.8 us -> 41.9 us
    unnamed x4 -> x1, local copies, waits for them, and re-layouts: 5.65 us -> 1.57 us
    pallas_call x1, Pallas kernels: 45.8 us -> 41.9 us  [per_device(): pl.pallas_call(functools.partial(layer_kernel, hi, lo), out_shape=(jax.Sh...]
    reshape x1 -> x0, local copies, waits for them, and re-layouts: 1.32 us -> none  [per_device(): new_expert.reshape(-1, 1)]
where the time goes in v2:
time: 46.3 us; the launch traced here: 46 us
  Pallas kernels  41.9 us (90%)
  between operations  2.45 us (5%)
  local copies, waits for them, and re-layouts  1.57 us (3%)
    pallas_call x1, Pallas kernels, per_device(): pl.pallas_call(functools.partial(layer_kernel, hi, lo), out_shape=(jax.Sh...  41.9 us
    unnamed x1, local copies, waits for them, and re-layouts  1.57 us

profile of v2, /device:TPU:0, one launch (start us, length us, event | category | flops | bytes accessed | tf_op | source)
XLA Modules:
  0.0 46.0 jit_solution(10603233908480726272)
XLA Ops:
  0.6 41.9 %expert_layer.1 = (bf16[2,16,2048]{2,1,0:T(8,128)(2,1)}, s32[1,1]{1,0:T(1,128)}) custom-call(bf16[2,16,2048]{2,1,0:T(8,128)(2,1)} %act_ref.1, f32[2,1,16]{2,1,0:T(1,128)} %bitcast.12, s32[2,1,16]{2,1,0:T(1,128)} %bitcast.13, s32[2,1,16]{2,1,0:T(1,128)} %bitcast.14, s32[1,8]{1,0:T(1,128)} %bitcast.15, s32[1,16]{1,0:T(1,128)} %bitcast.16, ...), custom_call_target="tpu_custom_call" | custom-call | flops 2415919104 | bytes 9437184 | tf_op jit(solution)/shard_map/expert_layer/pallas_call | solution.py:339
  42.6 1.6 %copy.16 = bf16[2,16,2048]{2,1,0:T(8,128)(2,1)} copy(bf16[2,16,2048]{2,1,0:T(8,128)(2,1)} %get-tuple-element.8) | data formatting | bytes 262144

commit v3 on v2

--- a/solution.py
+++ b/solution.py
@@ -36,6 +36,7 @@
     tok,
     wgu,
     wd,
+    hid,
     res,
     xbuf,
     comb,
@@ -198,15 +199,32 @@
     total = hi * lo * t
     step = min(ROWS, total)
 
-    def expert(g):
+    def chunks(body):
+        if total == step:
+            body(pl.ds(0, step))
+        else:
+
+            @pl.loop(0, total // step)
+            def _(i):
+                body(pl.ds(pl.multiple_of(i * step, step), step))
+
+    def hidden(g):
         def body(part):
             both = jnp.dot(
                 tok[g, part, pl.ds(0, width)], wgu[...], preferred_element_type=jnp.float32
             )
             gate, up = both[:, :full], both[:, full:]
-            hidden = (gate / (1.0 + jnp.exp(-gate)) * up).astype(jnp.bfloat16)
+            hid[g, part, :] = (gate / (1.0 + jnp.exp(-gate)) * up).astype(jnp.bfloat16)
+
+        chunks(body)
+
+    def result(g):
+        def body(part):
             value = lax.dot_general(
-                hidden, wd[...], (((1,), (1,)), ((), ())), preferred_element_type=jnp.float32
+                hid[g, part, :],
+                wd[...],
+                (((1,), (1,)), ((), ())),
+                preferred_element_type=jnp.float32,
             )
             value = value.astype(jnp.bfloat16).astype(jnp.float32)
             marks = tok[g, part, pl.ds(width, LANES)].astype(jnp.float32)
@@ -219,14 +237,7 @@
                 scale += jnp.where(home == chip.astype(jnp.float32), weight, 0.0)
             res[g, part, :] = (value * scale).astype(jnp.bfloat16)
 
-        if total == step:
-            body(pl.ds(0, step))
-        else:
-
-            @pl.loop(0, total // step)
-            def _(i):
-                body(pl.ds(pl.multiple_of(i * step, step), step))
-
+        chunks(body)
         for dz in back_order:
             for dx in range(1, lo):
                 pending.append(
@@ -268,6 +279,17 @@
             value += fin[g, dz].astype(jnp.float32)
         out_ref[g] = value.astype(jnp.bfloat16)
 
+    def await_panel(p):
+        panel_copies[p].wait()
+        first = pl.multiple_of((1 - core) * half, LANES)
+        if p == 0:
+            ref = wgu.at[:, pl.ds(first, half)]
+        elif p == 1:
+            ref = wgu.at[:, pl.ds(pl.multiple_of(full + first, LANES), half)]
+        else:
+            ref = wd.at[:, pl.ds(first, half)]
+        arrived(ref, panel_send.at[p], panel_recv.at[p])
+
     def picks_of(slot):
         count = jnp.zeros((1, 1), jnp.float32)
         for g in range(batches):
@@ -288,19 +310,16 @@
     for g in range(1, batches):
         send_z(g)
     await_x(0)
-    for p, (copy, (_, dst)) in enumerate(zip(panel_copies, panels)):
-        copy.wait()
-        other_cols = (
-            wgu.at[:, pl.ds(pl.multiple_of((1 - core) * half, LANES), half)],
-            wgu.at[:, pl.ds(pl.multiple_of(full + (1 - core) * half, LANES), half)],
-            wd.at[:, pl.ds(pl.multiple_of((1 - core) * half, LANES), half)],
-        )[p]
-        arrived(other_cols, panel_send.at[p], panel_recv.at[p])
     for g in range(batches):
+        if g == 0:
+            await_panel(0)
+            await_panel(1)
+        hidden(g)
+        if g == 0:
+            await_panel(2)
+        result(g)
         if g + 1 < batches:
             relay_z(g + 1)
-        expert(g)
-        if g + 1 < batches:
             await_x(g + 1)
         collect(g)
 
@@ -348,6 +367,7 @@
             pltpu.VMEM((batches, total, width + LANES), bf16),
             pltpu.VMEM((width, 4 * half), bf16),
             pltpu.VMEM((width, 2 * half), bf16),
+            pltpu.VMEM((batches, total, 2 * half), bf16),
             pltpu.VMEM((batches, total, width), bf16),
             pltpu.VMEM((batches, lo, hi, t, width), bf16),
             pltpu.VMEM((batches, hi, t, width), bf16),

time: 46.3 us -> 45.4 us (0.981)
  Pallas kernels: 41.9 us -> 41.2 us
    pallas_call x1, Pallas kernels: 41.9 us -> 41.2 us  [per_device(): pl.pallas_call(functools.partial(layer_kernel, hi, lo), out_shape=(jax.Sh...]
where the time goes in v3:
time: 45.4 us; the launch traced here: 45.2 us
  Pallas kernels  41.2 us (91%)
  between operations  2.45 us (5%)
  local copies, waits for them, and re-layouts  1.57 us (3%)
    pallas_call x1, Pallas kernels, per_device(): pl.pallas_call(functools.partial(layer_kernel, hi, lo), out_shape=(jax.Sh...  41.2 us
    unnamed x1, local copies, waits for them, and re-layouts  1.57 us

profile of v3, /device:TPU:0, one launch (start us, length us, event | category | flops | bytes accessed | tf_op | source)
XLA Modules:
  0.0 45.2 jit_solution(3904889174870158845)
XLA Ops:
  0.6 41.2 %expert_layer.1 = (bf16[2,16,2048]{2,1,0:T(8,128)(2,1)}, s32[1,1]{1,0:T(1,128)}) custom-call(bf16[2,16,2048]{2,1,0:T(8,128)(2,1)} %act_ref.1, f32[2,1,16]{2,1,0:T(1,128)} %bitcast.12, s32[2,1,16]{2,1,0:T(1,128)} %bitcast.13, s32[2,1,16]{2,1,0:T(1,128)} %bitcast.14, s32[1,8]{1,0:T(1,128)} %bitcast.15, s32[1,16]{1,0:T(1,128)} %bitcast.16, ...), custom_call_target="tpu_custom_call" | custom-call | flops 2415919104 | bytes 9437184 | tf_op jit(solution)/shard_map/expert_layer/pallas_call | solution.py:358
  41.8 1.6 %copy.16 = bf16[2,16,2048]{2,1,0:T(8,128)(2,1)} copy(bf16[2,16,2048]{2,1,0:T(8,128)(2,1)} %get-tuple-element.8) | data formatting | bytes 262144

commit v4 on v3

--- a/solution.py
+++ b/solution.py
@@ -164,37 +164,93 @@
 
     pending = []
 
-    def across(g, dz):
-        block = tok.at[g, rows(chip_at(-dz, 0))]
-        for dx in range(1, lo):
-            pending.append(
-                remote(
-                    block, block, x_send.at[g, dz, dx], x_recv.at[g, dz, dx], device_at(0, dx)
-                )
+    moves = [(2 * s - (sign < 0), sign, s) for s in range(1, hi) for sign in (-1, 1)]
+
+    def present(sign, s):
+        return zi >= s if sign < 0 else zi + s < hi
+
+    def onward(sign):
+        return zi + 1 < hi if sign < 0 else zi >= 1
+
+    def across(g, place, block):
+        return [
+            remote(
+                block, block, x_send.at[g, place, dx], x_recv.at[g, place, dx], device_at(0, dx)
+            )
+            for dx in range(1, lo)
+        ]
+
+    def send_on(g, block, sign, s):
+        place = 2 * s - (sign < 0)
+
+        @pl.when(onward(sign))
+        def _():
+            remote(
+                block,
+                block,
+                z_send.at[g, place],
+                z_recv.at[g, place],
+                device_at(-sign, 0),
             )
 
     def send_z(g):
         act_copies[g].wait()
         block = tok.at[g, rows(chip)]
-        for dz in range(1, hi):
-            pending.append(
-                remote(block, block, z_send.at[g, dz], z_recv.at[g, dz], device_at(dz, 0))
-            )
-        across(g, 0)
+        for sign in (-1, 1):
+            send_on(g, block, sign, 1)
+        across(g, 0, block)
 
     def relay_z(g):
-        for dz in range(1, hi):
-            arrived(tok.at[g, rows(chip_at(-dz, 0))], z_send.at[g, dz], z_recv.at[g, dz])
-            across(g, dz)
+        for place, sign, s in moves:
+
+            @pl.when(present(sign, s))
+            def _():
+                block = tok.at[g, rows((zi + sign * s) * lo + xi)]
+                arrived(block, z_send.at[g, place], z_recv.at[g, place])
+                if s + 1 < hi:
+                    send_on(g, block, sign, s + 1)
+                across(g, place, block)
 
     def await_x(g):
-        for dz in range(hi):
-            for dx in range(1, lo):
-                arrived(
-                    tok.at[g, rows(chip_at(-dz, -dx))],
-                    x_send.at[g, dz, dx],
-                    x_recv.at[g, dz, dx],
-                )
+        for dx in range(1, lo):
+            x = lax.rem(xi + lo - dx, lo)
+            arrived(tok.at[g, rows(zi * lo + x)], x_send.at[g, 0, dx], x_recv.at[g, 0, dx])
+        for place, sign, s in moves:
+
+            @pl.when(present(sign, s))
+            def _():
+                for dx in range(1, lo):
+                    x = lax.rem(xi + lo - dx, lo)
+                    arrived(
+                        tok.at[g, rows((zi + sign * s) * lo + x)],
+                        x_send.at[g, place, dx],
+                        x_recv.at[g, place, dx],
+                    )
+
+    def sent(ref, send, recv):
+        pltpu.make_async_remote_copy(
+            src_ref=ref,
+            dst_ref=ref,
+            send_sem=send,
+            recv_sem=recv,
+            device_id={"expert": sibling},
+            device_id_type=MESH,
+        ).wait_send()
+
+    def await_sent(g):
+        block = tok.at[g, rows(chip)]
+        for dx in range(1, lo):
+            sent(block, x_send.at[g, 0, dx], x_recv.at[g, 0, dx])
+        for place, sign, s in moves:
+
+            @pl.when(present(sign, s))
+            def _():
+                for dx in range(1, lo):
+                    sent(block, x_send.at[g, place, dx], x_recv.at[g, place, dx])
+
+            @pl.when(present(sign, s - 1) & onward(sign))
+            def _():
+                sent(block, z_send.at[g, place], z_recv.at[g, place])
 
     total = hi * lo * t
     step = min(ROWS, total)
@@ -331,6 +387,8 @@
         finish(g)
     arrived(tally.at[1], tally_sem.at[0], tally_sem.at[1])
     load_ref[...] = (count + tally[1, :1, :1]).astype(jnp.int32)
+    for g in range(batches):
+        await_sent(g)
     for copy in pending:
         copy.wait_send()
 
@@ -376,10 +434,10 @@
             dma((batches + 3,)),
             dma((3,)),
             dma((3,)),
-            dma((batches, hi)),
-            dma((batches, hi)),
-            dma((batches, hi, lo)),
-            dma((batches, hi, lo)),
+            dma((batches, 2 * hi - 1)),
+            dma((batches, 2 * hi - 1)),
+            dma((batches, 2 * hi - 1, lo)),
+            dma((batches, 2 * hi - 1, lo)),
             dma((batches, hi, lo)),
             dma((batches, hi, lo)),
             dma((batches, hi)),

time: 45.4 us -> 46.4 us (1.022)
  Pallas kernels: 41.2 us -> 42.2 us
    pallas_call x1, Pallas kernels: 41.2 us -> 42.2 us  [per_device(): pl.pallas_call(functools.partial(layer_kernel, hi, lo), out_shape=(jax.Sh...]
where the time goes in v4:
time: 46.4 us; the launch traced here: 46.2 us
  Pallas kernels  42.2 us (91%)
  between operations  2.45 us (5%)
  local copies, waits for them, and re-layouts  1.57 us (3%)
    pallas_call x1, Pallas kernels, per_device(): pl.pallas_call(functools.partial(layer_kernel, hi, lo), out_shape=(jax.Sh...  42.2 us
    unnamed x1, local copies, waits for them, and re-layouts  1.57 us

profile of v4, /device:TPU:0, one launch (start us, length us, event | category | flops | bytes accessed | tf_op | source)
XLA Modules:
  0.0 46.2 jit_solution(5519426968816877772)
XLA Ops:
  0.6 42.2 %expert_layer.1 = (bf16[2,16,2048]{2,1,0:T(8,128)(2,1)}, s32[1,1]{1,0:T(1,128)}) custom-call(bf16[2,16,2048]{2,1,0:T(8,128)(2,1)} %act_ref.1, f32[2,1,16]{2,1,0:T(1,128)} %bitcast.12, s32[2,1,16]{2,1,0:T(1,128)} %bitcast.13, s32[2,1,16]{2,1,0:T(1,128)} %bitcast.14, s32[1,8]{1,0:T(1,128)} %bitcast.15, s32[1,16]{1,0:T(1,128)} %bitcast.16, ...), custom_call_target="tpu_custom_call" | custom-call | flops 2415919104 | bytes 9437184 | tf_op jit(solution)/shard_map/expert_layer/pallas_call | solution.py:416
  42.8 1.6 %copy.16 = bf16[2,16,2048]{2,1,0:T(8,128)(2,1)} copy(bf16[2,16,2048]{2,1,0:T(8,128)(2,1)} %get-tuple-element.8) | data formatting | bytes 262144

commit v5 on v3

--- a/solution.py
+++ b/solution.py
@@ -11,6 +11,7 @@
 MESH = pl.DeviceIdType.MESH
 LANES = 128
 ROWS = 256
+PARTS = 4
 
 
 def grid_of(devices):
@@ -59,6 +60,7 @@
     top = ids_ref.shape[1]
     half = gate_ref.shape[2]
     full = 2 * half
+    piece = width // PARTS
     me = lax.axis_index("expert")
     core = lax.rem(me, 2)
     chip = me // 2
@@ -288,7 +290,8 @@
             ref = wgu.at[:, pl.ds(pl.multiple_of(full + first, LANES), half)]
         else:
             ref = wd.at[:, pl.ds(first, half)]
-        arrived(ref, panel_send.at[p], panel_recv.at[p])
+        for q in range(PARTS):
+            arrived(ref.at[pl.ds(q * piece, piece)], panel_send.at[p, q], panel_recv.at[p, q])
 
     def picks_of(slot):
         count = jnp.zeros((1, 1), jnp.float32)
@@ -301,11 +304,18 @@
         return count
 
     send_z(0)
-    pushed = [
-        remote(src, dst, panel_send.at[p], panel_recv.at[p], sibling)
-        for p, (src, dst) in enumerate(panels)
-    ]
-    pending.extend(pushed)
+    for p, (src, dst) in enumerate(panels):
+        for q in range(PARTS):
+            part = pl.ds(q * piece, piece)
+            pending.append(
+                remote(
+                    src.at[part],
+                    dst.at[part],
+                    panel_send.at[p, q],
+                    panel_recv.at[p, q],
+                    sibling,
+                )
+            )
     relay_z(0)
     for g in range(1, batches):
         send_z(g)
@@ -374,8 +384,8 @@
             pltpu.VMEM((batches, hi, t, width), bf16),
             pltpu.VMEM((2, 8, LANES), jnp.float32),
             dma((batches + 3,)),
-            dma((3,)),
-            dma((3,)),
+            dma((3, PARTS)),
+            dma((3, PARTS)),
             dma((batches, hi)),
             dma((batches, hi)),
             dma((batches, hi, lo)),

time: 45.4 us -> 45.6 us (level)
  no operation moved by 1% of the time
where the time goes in v5:
time: 45.6 us; the launch traced here: 45.4 us
  Pallas kernels  41.4 us (91%)
  between operations  2.45 us (5%)
  local copies, waits for them, and re-layouts  1.57 us (3%)
    pallas_call x1, Pallas kernels, per_device(): pl.pallas_call(functools.partial(layer_kernel, hi, lo), out_shape=(jax.Sh...  41.4 us
    unnamed x1, local copies, waits for them, and re-layouts  1.57 us

profile of v5, /device:TPU:0, one launch (start us, length us, event | category | flops | bytes accessed | tf_op | source)
XLA Modules:
  0.0 45.4 jit_solution(14227548056080994240)
XLA Ops:
  0.6 41.4 %expert_layer.1 = (bf16[2,16,2048]{2,1,0:T(8,128)(2,1)}, s32[1,1]{1,0:T(1,128)}) custom-call(bf16[2,16,2048]{2,1,0:T(8,128)(2,1)} %act_ref.1, f32[2,1,16]{2,1,0:T(1,128)} %bitcast.12, s32[2,1,16]{2,1,0:T(1,128)} %bitcast.13, s32[2,1,16]{2,1,0:T(1,128)} %bitcast.14, s32[1,8]{1,0:T(1,128)} %bitcast.15, s32[1,16]{1,0:T(1,128)} %bitcast.16, ...), custom_call_target="tpu_custom_call" | custom-call | flops 2415919104 | bytes 9437184 | tf_op jit(solution)/shard_map/expert_layer/pallas_call | solution.py:368
  42.0 1.6 %copy.16 = bf16[2,16,2048]{2,1,0:T(8,128)(2,1)} copy(bf16[2,16,2048]{2,1,0:T(8,128)(2,1)} %get-tuple-element.8) | data formatting | bytes 262144

commit v6 on v5

--- a/solution.py
+++ b/solution.py
@@ -37,6 +37,7 @@
     tok,
     wgu,
     wd,
+    stage,
     hid,
     res,
     xbuf,
@@ -117,7 +118,7 @@
     panels = (
         (gate_ref.at[0], wgu.at[:, gate_cols]),
         (up_ref.at[0], wgu.at[:, up_cols]),
-        (down_ref.at[0], wd.at[:, gate_cols]),
+        (down_ref.at[0], stage),
     )
     act_copies = [
         local(act_ref.at[g], tok.at[g, rows(chip), pl.ds(0, width)], local_sem.at[g])
@@ -222,12 +223,7 @@
 
     def result(g):
         def body(part):
-            value = lax.dot_general(
-                hid[g, part, :],
-                wd[...],
-                (((1,), (1,)), ((), ())),
-                preferred_element_type=jnp.float32,
-            )
+            value = jnp.dot(hid[g, part, :], wd[...], preferred_element_type=jnp.float32)
             value = value.astype(jnp.bfloat16).astype(jnp.float32)
             marks = tok[g, part, pl.ds(width, LANES)].astype(jnp.float32)
             scale = jnp.zeros((step, 1), jnp.float32)
@@ -282,16 +278,15 @@
         out_ref[g] = value.astype(jnp.bfloat16)
 
     def await_panel(p):
+        first = pl.multiple_of((1 - core) * half, LANES)
+        if p == 2:
+            arrived(wd.at[pl.ds(first, half)], panel_send.at[2, 0], panel_recv.at[2, 0])
+            return
         panel_copies[p].wait()
-        first = pl.multiple_of((1 - core) * half, LANES)
-        if p == 0:
-            ref = wgu.at[:, pl.ds(first, half)]
-        elif p == 1:
-            ref = wgu.at[:, pl.ds(pl.multiple_of(full + first, LANES), half)]
-        else:
-            ref = wd.at[:, pl.ds(first, half)]
+        other_cols = pl.ds(pl.multiple_of(p * full + first, LANES), half)
         for q in range(PARTS):
-            arrived(ref.at[pl.ds(q * piece, piece)], panel_send.at[p, q], panel_recv.at[p, q])
+            part = pl.ds(q * piece, piece)
+            arrived(wgu.at[part, other_cols], panel_send.at[p, q], panel_recv.at[p, q])
 
     def picks_of(slot):
         count = jnp.zeros((1, 1), jnp.float32)
@@ -304,7 +299,7 @@
         return count
 
     send_z(0)
-    for p, (src, dst) in enumerate(panels):
+    for p, (src, dst) in enumerate(panels[:2]):
         for q in range(PARTS):
             part = pl.ds(q * piece, piece)
             pending.append(
@@ -316,6 +311,16 @@
                     sibling,
                 )
             )
+    panel_copies[2].wait()
+    tall = min(ROWS, width)
+
+    @pl.loop(0, width // tall)
+    def _(i):
+        part = pl.ds(pl.multiple_of(i * tall, tall), tall)
+        wd[gate_cols, part] = stage[part, :].T
+
+    turned = wd.at[gate_cols]
+    pending.append(remote(turned, turned, panel_send.at[2, 0], panel_recv.at[2, 0], sibling))
     relay_z(0)
     for g in range(1, batches):
         send_z(g)
@@ -376,7 +381,8 @@
         scratch_shapes=[
             pltpu.VMEM((batches, total, width + LANES), bf16),
             pltpu.VMEM((width, 4 * half), bf16),
-            pltpu.VMEM((width, 2 * half), bf16),
+            pltpu.VMEM((2 * half, width), bf16),
+            pltpu.VMEM((width, half), bf16),
             pltpu.VMEM((batches, total, 2 * half), bf16),
             pltpu.VMEM((batches, total, width), bf16),
             pltpu.VMEM((batches, lo, hi, t, width), bf16),

time: 45.6 us -> 44.5 us (0.976)
  Pallas kernels: 41.4 us -> 40.3 us
    pallas_call x1, Pallas kernels: 41.4 us -> 40.3 us  [per_device(): pl.pallas_call(functools.partial(layer_kernel, hi, lo), out_shape=(jax.Sh...]
where the time goes in v6:
time: 44.5 us; the launch traced here: 44.3 us
  Pallas kernels  40.3 us (91%)
  between operations  2.45 us (6%)
  local copies, waits for them, and re-layouts  1.57 us (4%)
    pallas_call x1, Pallas kernels, per_device(): pl.pallas_call(functools.partial(layer_kernel, hi, lo), out_shape=(jax.Sh...  40.3 us
    unnamed x1, local copies, waits for them, and re-layouts  1.57 us

profile of v6, /device:TPU:0, one launch (start us, length us, event | category | flops | bytes accessed | tf_op | source)
XLA Modules:
  0.0 44.3 jit_solution(1623441543185160864)
XLA Ops:
  0.6 40.3 %expert_layer.1 = (bf16[2,16,2048]{2,1,0:T(8,128)(2,1)}, s32[1,1]{1,0:T(1,128)}) custom-call(bf16[2,16,2048]{2,1,0:T(8,128)(2,1)} %act_ref.1, f32[2,1,16]{2,1,0:T(1,128)} %bitcast.12, s32[2,1,16]{2,1,0:T(1,128)} %bitcast.13, s32[2,1,16]{2,1,0:T(1,128)} %bitcast.14, s32[1,8]{1,0:T(1,128)} %bitcast.15, s32[1,16]{1,0:T(1,128)} %bitcast.16, ...), custom_call_target="tpu_custom_call" | custom-call | flops 2415919104 | bytes 9437184 | tf_op jit(solution)/shard_map/expert_layer/pallas_call | solution.py:373
  40.9 1.6 %copy.16 = bf16[2,16,2048]{2,1,0:T(8,128)(2,1)} copy(bf16[2,16,2048]{2,1,0:T(8,128)(2,1)} %get-tuple-element.8) | data formatting | bytes 262144

commit v7 on v6

--- a/solution.py
+++ b/solution.py
@@ -11,7 +11,8 @@
 MESH = pl.DeviceIdType.MESH
 LANES = 128
 ROWS = 256
-PARTS = 4
+PARTS = 8
+DOWN_PARTS = 4
 
 
 def grid_of(devices):
@@ -62,6 +63,7 @@
     half = gate_ref.shape[2]
     full = 2 * half
     piece = width // PARTS
+    strip = half // DOWN_PARTS
     me = lax.axis_index("expert")
     core = lax.rem(me, 2)
     chip = me // 2
@@ -80,13 +82,16 @@
     def rows(place):
         return pl.ds(pl.multiple_of(place * t, t), t)
 
-    def remote(src, dst, send, recv, device):
+    groups = lax.axis_size("groups")
+    group = lax.axis_index("groups")
+
+    def remote(src, dst, send, recv, device, turn=0):
         copy = pltpu.make_async_remote_copy(
             src_ref=src,
             dst_ref=dst,
             send_sem=send,
             recv_sem=recv,
-            device_id={"expert": device},
+            device_id={"groups": lax.rem(group + turn, groups), "expert": device},
             device_id_type=MESH,
         )
         copy.start()
@@ -112,6 +117,11 @@
     barrier = pltpu.get_barrier_semaphore()
     for peer in peers:
         pl.semaphore_signal(barrier, inc=1, device_id={"expert": peer}, device_id_type=MESH)
+
+    turns = sorted({1 % groups, (groups - 1) % groups} - {0})
+    for turn in turns:
+        other = {"groups": lax.rem(group + turn, groups), "expert": sibling}
+        pl.semaphore_signal(barrier, inc=1, device_id=other, device_id_type=MESH)
 
     gate_cols = pl.ds(pl.multiple_of(core * half, LANES), half)
     up_cols = pl.ds(pl.multiple_of(full + core * half, LANES), half)
@@ -163,7 +173,7 @@
                 marks = jnp.where(lane == place * top + k, part, marks)
         tok[g, rows(chip), pl.ds(width, LANES)] = marks.astype(jnp.bfloat16)
 
-    pl.semaphore_wait(barrier, len(peers))
+    pl.semaphore_wait(barrier, len(peers) + len(turns))
 
     pending = []
 
@@ -280,7 +290,9 @@
     def await_panel(p):
         first = pl.multiple_of((1 - core) * half, LANES)
         if p == 2:
-            arrived(wd.at[pl.ds(first, half)], panel_send.at[2, 0], panel_recv.at[2, 0])
+            for q in range(DOWN_PARTS):
+                part = pl.ds(pl.multiple_of((1 - core) * half + q * strip, 16), strip)
+                arrived(wd.at[part], panel_send.at[2, q], panel_recv.at[2, q])
             return
         panel_copies[p].wait()
         other_cols = pl.ds(pl.multiple_of(p * full + first, LANES), half)
@@ -309,6 +321,7 @@
                     panel_send.at[p, q],
                     panel_recv.at[p, q],
                     sibling,
+                    turn=int(q == 0),
                 )
             )
     panel_copies[2].wait()
@@ -319,8 +332,18 @@
         part = pl.ds(pl.multiple_of(i * tall, tall), tall)
         wd[gate_cols, part] = stage[part, :].T
 
-    turned = wd.at[gate_cols]
-    pending.append(remote(turned, turned, panel_send.at[2, 0], panel_recv.at[2, 0], sibling))
+    for q in range(DOWN_PARTS):
+        turned = wd.at[pl.ds(pl.multiple_of(core * half + q * strip, 16), strip)]
+        pending.append(
+            remote(
+                turned,
+                turned,
+                panel_send.at[2, q],
+                panel_recv.at[2, q],
+                sibling,
+                turn=int(q == 0),
+            )
+        )
     relay_z(0)
     for g in range(1, batches):
         send_z(g)

time: 44.5 us -> 55.2 us (1.24)
  Pallas kernels: 40.3 us -> 51 us
    pallas_call x1, Pallas kernels: 40.3 us -> 51 us  [per_device(): pl.pallas_call(functools.partial(layer_kernel, hi, lo), out_shape=(jax.Sh...]
where the time goes in v7:
time: 55.2 us; the launch traced here: 55 us
  Pallas kernels  51 us (92%)
  between operations  2.45 us (4%)
  local copies, waits for them, and re-layouts  1.57 us (3%)
    pallas_call x1, Pallas kernels, per_device(): pl.pallas_call(functools.partial(layer_kernel, hi, lo), out_shape=(jax.Sh...  51 us
    unnamed x1, local copies, waits for them, and re-layouts  1.57 us

profile of v7, /device:TPU:0, one launch (start us, length us, event | category | flops | bytes accessed | tf_op | source)
XLA Modules:
  0.0 55.0 jit_solution(2173240050443551997)
XLA Ops:
  0.6 51.0 %expert_layer.1 = (bf16[2,16,2048]{2,1,0:T(8,128)(2,1)}, s32[1,1]{1,0:T(1,128)}) custom-call(bf16[2,16,2048]{2,1,0:T(8,128)(2,1)} %act_ref.1, f32[2,1,16]{2,1,0:T(1,128)} %bitcast.12, s32[2,1,16]{2,1,0:T(1,128)} %bitcast.13, s32[2,1,16]{2,1,0:T(1,128)} %bitcast.14, s32[1,8]{1,0:T(1,128)} %bitcast.15, s32[1,16]{1,0:T(1,128)} %bitcast.16, ...), custom_call_target="tpu_custom_call" | custom-call | flops 2415919104 | bytes 9437184 | tf_op jit(solution)/shard_map/expert_layer/pallas_call | solution.py:396
  51.6 1.6 %copy.16 = bf16[2,16,2048]{2,1,0:T(8,128)(2,1)} copy(bf16[2,16,2048]{2,1,0:T(8,128)(2,1)} %get-tuple-element.8) | data formatting | bytes 262144

commit v8 on v6

--- a/solution.py
+++ b/solution.py
@@ -42,7 +42,6 @@
     res,
     xbuf,
     comb,
-    fin,
     tally,
     local_sem,
     panel_send,
@@ -256,26 +255,26 @@
             for dx in range(1, lo):
                 arrived(xbuf.at[g, dx, dz], rx_send.at[g, dz, dx], rx_recv.at[g, dz, dx])
                 value += xbuf[g, dx, dz].astype(jnp.float32)
+            comb[g, dz] = value.astype(jnp.bfloat16)
             if dz:
-                comb[g, dz] = value.astype(jnp.bfloat16)
                 pending.append(
                     remote(
                         comb.at[g, dz],
-                        fin.at[g, dz],
+                        out_ref.at[dz, g],
                         rz_send.at[g, dz],
                         rz_recv.at[g, dz],
                         device_at(dz, 0),
                     )
                 )
             else:
-                fin[g, 0] = value.astype(jnp.bfloat16)
+                own_copies.append(local(comb.at[g, 0], out_ref.at[0, g], rz_send.at[g, 0]))
+
+    own_copies = []
 
     def finish(g):
-        value = fin[g, 0].astype(jnp.float32)
+        own_copies[g].wait()
         for dz in range(1, hi):
-            arrived(fin.at[g, dz], rz_send.at[g, dz], rz_recv.at[g, dz])
-            value += fin[g, dz].astype(jnp.float32)
-        out_ref[g] = value.astype(jnp.bfloat16)
+            arrived(out_ref.at[dz, g], rz_send.at[g, dz], rz_recv.at[g, dz])
 
     def await_panel(p):
         first = pl.multiple_of((1 - core) * half, LANES)
@@ -370,14 +369,14 @@
     vmem = pl.BlockSpec(memory_space=pltpu.VMEM)
     hbm = pl.BlockSpec(memory_space=pl.ANY)
     bf16 = jnp.bfloat16
-    out, load = pl.pallas_call(
+    parts, load = pl.pallas_call(
         functools.partial(layer_kernel, hi, lo),
         out_shape=(
-            jax.ShapeDtypeStruct(activations.shape, bf16),
+            jax.ShapeDtypeStruct((hi,) + activations.shape, bf16),
             jax.ShapeDtypeStruct((1, 1), jnp.int32),
         ),
         in_specs=[hbm, vmem, vmem, vmem, vmem, vmem, hbm, hbm, hbm],
-        out_specs=(vmem, vmem),
+        out_specs=(hbm, vmem),
         scratch_shapes=[
             pltpu.VMEM((batches, total, width + LANES), bf16),
             pltpu.VMEM((width, 4 * half), bf16),
@@ -386,7 +385,6 @@
             pltpu.VMEM((batches, total, 2 * half), bf16),
             pltpu.VMEM((batches, total, width), bf16),
             pltpu.VMEM((batches, lo, hi, t, width), bf16),
-            pltpu.VMEM((batches, hi, t, width), bf16),
             pltpu.VMEM((batches, hi, t, width), bf16),
             pltpu.VMEM((2, 8, LANES), jnp.float32),
             dma((batches + 3,)),
@@ -422,6 +420,7 @@
         up_panel,
         down_panel,
     )
+    out = jnp.sum(parts.astype(jnp.float32), axis=0).astype(bf16)
     return out, load.reshape(1)
 
 

time: 44.5 us -> 44.8 us (level)
  other arithmetic: 0 us -> 1.81 us
  local copies, waits for them, and re-layouts: 1.57 us -> 0 us
    reduce_sum x0 -> x1, other arithmetic: none -> 1.81 us  [per_device(): out = jnp.sum(parts.astype(jnp.float32), axis=0).astype(bf16)]
    unnamed x1 -> x0, local copies, waits for them, and re-layouts: 1.57 us -> none
where the time goes in v8:
time: 44.8 us; the launch traced here: 44.6 us
  Pallas kernels  40.3 us (90%)
  between operations  2.46 us (5%)
  other arithmetic  1.81 us (4%)
    pallas_call x1, Pallas kernels, per_device(): pl.pallas_call(functools.partial(layer_kernel, hi, lo), out_shape=(jax.Sh...  40.3 us
    reduce_sum x1, other arithmetic, per_device(): out = jnp.sum(parts.astype(jnp.float32), axis=0).astype(bf16)  1.81 us

profile of v8, /device:TPU:0, one launch (start us, length us, event | category | flops | bytes accessed | tf_op | source)
XLA Modules:
  0.0 44.6 jit_solution(1510113708386007653)
XLA Ops:
  0.6 40.3 %expert_layer.1 = (bf16[4,2,16,2048]{3,2,1,0:T(8,128)(2,1)}, s32[1,1]{1,0:T(1,128)}) custom-call(bf16[2,16,2048]{2,1,0:T(8,128)(2,1)} %act_ref.1, f32[2,1,16]{2,1,0:T(1,128)} %bitcast.12, s32[2,1,16]{2,1,0:T(1,128)} %bitcast.13, s32[2,1,16]{2,1,0:T(1,128)} %bitcast.14, s32[1,8]{1,0:T(1,128)} %bitcast.15, s32[1,16]{1,0:T(1,128)} %bitcast.16, ...), custom_call_target="tpu_custom_call" | custom-call | flops 2415919104 | bytes 9437184 | tf_op jit(solution)/shard_map/expert_layer/pallas_call | solution.py:372
  41.0 1.8 %reduce_sum.12 = bf16[2,16,2048]{2,1,0:T(8,128)(2,1)} reduce(bf16[4,2,16,2048]{3,2,1,0:T(8,128)(2,1)} %get-tuple-element.4, bf16[]{:T(256)} %constant.2.clone.1), dimensions={0}, to_apply=%region_0.0 | reduce | flops 196608 | bytes 655362 | tf_op jit(solution)/shard_map/reduce_sum | solution.py:423

commit v9 on v6

--- a/solution.py
+++ b/solution.py
@@ -336,6 +336,7 @@
         if g + 1 < batches:
             relay_z(g + 1)
             await_x(g + 1)
+    for g in range(batches):
         collect(g)
 
     tally[0] = jnp.broadcast_to(picks_of(sibling), tally.shape[1:])

time: 44.5 us -> 45.3 us (1.018)
  Pallas kernels: 40.3 us -> 41 us
    pallas_call x1, Pallas kernels: 40.3 us -> 41 us  [per_device(): pl.pallas_call(functools.partial(layer_kernel, hi, lo), out_shape=(jax.Sh...]
where the time goes in v9:
time: 45.3 us; the launch traced here: 45.1 us
  Pallas kernels  41 us (91%)
  between operations  2.45 us (5%)
  local copies, waits for them, and re-layouts  1.57 us (3%)
    pallas_call x1, Pallas kernels, per_device(): pl.pallas_call(functools.partial(layer_kernel, hi, lo), out_shape=(jax.Sh...  41 us
    unnamed x1, local copies, waits for them, and re-layouts  1.57 us

profile of v9, /device:TPU:0, one launch (start us, length us, event | category | flops | bytes accessed | tf_op | source)
XLA Modules:
  0.0 45.1 jit_solution(17888376757843071786)
XLA Ops:
  0.6 41.0 %expert_layer.1 = (bf16[2,16,2048]{2,1,0:T(8,128)(2,1)}, s32[1,1]{1,0:T(1,128)}) custom-call(bf16[2,16,2048]{2,1,0:T(8,128)(2,1)} %act_ref.1, f32[2,1,16]{2,1,0:T(1,128)} %bitcast.12, s32[2,1,16]{2,1,0:T(1,128)} %bitcast.13, s32[2,1,16]{2,1,0:T(1,128)} %bitcast.14, s32[1,8]{1,0:T(1,128)} %bitcast.15, s32[1,16]{1,0:T(1,128)} %bitcast.16, ...), custom_call_target="tpu_custom_call" | custom-call | flops 2415919104 | bytes 9437184 | tf_op jit(solution)/shard_map/expert_layer/pallas_call | solution.py:374
  41.7 1.6 %copy.16 = bf16[2,16,2048]{2,1,0:T(8,128)(2,1)} copy(bf16[2,16,2048]{2,1,0:T(8,128)(2,1)} %get-tuple-element.8) | data formatting | bytes 262144
